TPU v7x, 32 devices: a whole 2x2x4 slice. The times are simulated.
32 devices in a mesh: dp: 2 (over x), slab: 16 (over z, y, core).
Axes of the slice: x: 2, y: 2, z: 4, core: 2. Of those that a mesh axis runs over, the one named last changes fastest.
Arguments:
- field: float32 [2, 32, 128, 128, 128], P('dp', None, 'slab'), may hold values from -6 to 6
- cotangent: float32 [2, 32, 128, 128, 128], P('dp', None, 'slab'), may hold values from -6 to 6
- spec_weight: float32 [2, 32, 512, 1024], P(None, None, 'slab'), may hold values from -8 to 8
- bypass_weight: float32 [32, 32], replicated, may hold values from -1 to 1
Outputs:
- layer_out: float32 [2, 32, 128, 128, 128], P('dp', None, 'slab')
- grad_field: float32 [2, 32, 128, 128, 128], P('dp', None, 'slab')
- grad_spec: float32 [2, 32, 512, 1024], P(None, None, 'slab')
All inputs are finite; a program needn't handle non-finite values.
Results may differ from a plain program's by a relative error of at most 0.0001.
Values sent between devices are 32-bit elements; how exact they have to be, the bound alone decides.
No kernel may reach another device: no remote copies, remote signals or barrier semaphores. Data moves between devices by JAX's collectives and lax.ppermute only.
A program may use at most 384 MiB of HBM per device.

v0:
```python
import math
import jax
import jax.numpy as jnp
from jax import lax
from jax.sharding import PartitionSpec as P

GX = 128
GY = 128
GZ = 128
KX = 32
KY = 32
KZ = 16
precise = lax.Precision.HIGHEST


def wave_tables(length, count, signed):
    positions = jnp.arange(length, dtype=jnp.int32)
    indices = jnp.arange(count, dtype=jnp.int32)
    if signed:
        freqs = jnp.where(indices < count // 2, indices, indices - count)
    else:
        freqs = indices
    phase = positions[:, None] * freqs[None, :] % length
    angle = phase.astype(jnp.float32) * (2.0 * math.pi / length)
    return (jnp.cos(angle), jnp.sin(angle))


def gelu_exact(values):
    return jax.nn.gelu(values, approximate=False)


def plane_spectrum(data, weight, z_cos, z_sin, y_cos, y_sin):
    chans, planes = (data.shape[0], data.shape[1])
    part_re = jnp.einsum("cxyz,zk->cxky", data, z_cos, precision=precise)
    part_im = -jnp.einsum("cxyz,zk->cxky", data, z_sin, precision=precise)
    mid_re = jnp.einsum("cxky,yj->cxjk", part_re, y_cos, precision=precise) + jnp.einsum(
        "cxky,yj->cxjk", part_im, y_sin, precision=precise
    )
    mid_im = jnp.einsum("cxky,yj->cxjk", part_im, y_cos, precision=precise) - jnp.einsum(
        "cxky,yj->cxjk", part_re, y_sin, precision=precise
    )
    stacked = jnp.stack([mid_re * weight, mid_im * weight])
    return stacked.reshape(2, chans, planes, KY * KZ)


def along_first(moved, x_cos, x_sin):
    line_re, line_im = (moved[0], moved[1])
    full_re = jnp.einsum("cxp,xi->cpi", line_re, x_cos, precision=precise) + jnp.einsum(
        "cxp,xi->cpi", line_im, x_sin, precision=precise
    )
    full_im = jnp.einsum("cxp,xi->cpi", line_im, x_cos, precision=precise) - jnp.einsum(
        "cxp,xi->cpi", line_re, x_sin, precision=precise
    )
    return (full_re, full_im)


def back_first(spec_re, spec_im, x_cos, x_sin):
    wide_re = jnp.einsum("cpi,xi->cxp", spec_re, x_cos, precision=precise) - jnp.einsum(
        "cpi,xi->cxp", spec_im, x_sin, precision=precise
    )
    wide_im = jnp.einsum("cpi,xi->cxp", spec_re, x_sin, precision=precise) + jnp.einsum(
        "cpi,xi->cxp", spec_im, x_cos, precision=precise
    )
    return jnp.stack([wide_re, wide_im])


def plane_inverse(arrived, weight, z_cos, z_sin, y_cos, y_sin):
    chans, planes = (arrived.shape[1], arrived.shape[2])
    shaped = arrived.reshape(2, chans, planes, KY, KZ)
    wide_re, wide_im = (shaped[0], shaped[1])
    plane_re = jnp.einsum("cxjk,yj->cxky", wide_re, y_cos, precision=precise) - jnp.einsum(
        "cxjk,yj->cxky", wide_im, y_sin, precision=precise
    )
    plane_im = jnp.einsum("cxjk,yj->cxky", wide_re, y_sin, precision=precise) + jnp.einsum(
        "cxjk,yj->cxky", wide_im, y_cos, precision=precise
    )
    plane_re = plane_re * weight[:, None]
    plane_im = plane_im * weight[:, None]
    return jnp.einsum("cxky,zk->cxyz", plane_re, z_cos, precision=precise) - jnp.einsum(
        "cxky,zk->cxyz", plane_im, z_sin, precision=precise
    )


def on_device(field, cotangent, spec_weight, bypass_weight):
    count = lax.axis_size("slab")
    pairs = KY * KZ // count
    chans = field.shape[1]
    z_cos, z_sin = wave_tables(GZ, KZ, False)
    y_cos, y_sin = wave_tables(GY, KY, True)
    x_cos, x_sin = wave_tables(GX, KX, True)
    kz_index = jnp.arange(KZ, dtype=jnp.int32)
    fold = jnp.where(kz_index == 0, 1.0, 2.0).astype(jnp.float32) / float(GX * GY * GZ)
    ones = jnp.ones((KZ,), jnp.float32)
    weights = spec_weight.reshape(2, chans, pairs, KX, chans)
    w_real = weights[0]
    w_imag = weights[1]
    source = field[0]
    local_spec = plane_spectrum(source, ones, z_cos, z_sin, y_cos, y_sin)
    moved = lax.all_to_all(local_spec, "slab", split_axis=3, concat_axis=2, tiled=True)
    hat_re, hat_im = along_first(moved, x_cos, x_sin)
    mix_re = jnp.einsum("cpi,cpio->opi", hat_re, w_real, precision=precise) - jnp.einsum(
        "cpi,cpio->opi", hat_im, w_imag, precision=precise
    )
    mix_im = jnp.einsum("cpi,cpio->opi", hat_re, w_imag, precision=precise) + jnp.einsum(
        "cpi,cpio->opi", hat_im, w_real, precision=precise
    )
    outgoing = back_first(mix_re, mix_im, x_cos, x_sin)
    arrived = lax.all_to_all(outgoing, "slab", split_axis=2, concat_axis=3, tiled=True)
    spectral = plane_inverse(arrived, fold, z_cos, z_sin, y_cos, y_sin)
    pre = spectral + jnp.einsum("co,cxyz->oxyz", bypass_weight, source, precision=precise)
    result, pullback = jax.vjp(gelu_exact, pre)
    grad_pre = pullback(cotangent[0])[0]
    fold_grid = jnp.broadcast_to(fold, (KY, KZ))
    cot_spec = plane_spectrum(grad_pre, fold_grid, z_cos, z_sin, y_cos, y_sin)
    cot_moved = lax.all_to_all(cot_spec, "slab", split_axis=3, concat_axis=2, tiled=True)
    grad_re, grad_im = along_first(cot_moved, x_cos, x_sin)
    own_real = jnp.einsum("cpi,opi->cpio", hat_re, grad_re, precision=precise) + jnp.einsum(
        "cpi,opi->cpio", hat_im, grad_im, precision=precise
    )
    own_imag = jnp.einsum("cpi,opi->cpio", hat_re, grad_im, precision=precise) - jnp.einsum(
        "cpi,opi->cpio", hat_im, grad_re, precision=precise
    )
    summed = lax.psum(jnp.stack([own_real, own_imag]), "dp")
    grad_spec = summed.reshape(2, chans, pairs, KX * chans)
    input_re = jnp.einsum("opi,cpio->cpi", grad_re, w_real, precision=precise) + jnp.einsum(
        "opi,cpio->cpi", grad_im, w_imag, precision=precise
    )
    input_im = jnp.einsum("opi,cpio->cpi", grad_im, w_real, precision=precise) - jnp.einsum(
        "opi,cpio->cpi", grad_re, w_imag, precision=precise
    )
    grad_out = back_first(input_re, input_im, x_cos, x_sin)
    grad_arrived = lax.all_to_all(grad_out, "slab", split_axis=2, concat_axis=3, tiled=True)
    back_field = plane_inverse(grad_arrived, ones, z_cos, z_sin, y_cos, y_sin)
    back_field = back_field + jnp.einsum(
        "co,oxyz->cxyz", bypass_weight, grad_pre, precision=precise
    )
    return (result[None], back_field[None], grad_spec)


def solution(mesh):
    in_specs = (
        P("dp", None, "slab", None, None),
        P("dp", None, "slab", None, None),
        P(None, None, "slab", None),
        P(),
    )
    out_specs = (
        P("dp", None, "slab", None, None),
        P("dp", None, "slab", None, None),
        P(None, None, "slab", None),
    )
    return jax.shard_map(
        on_device, mesh=mesh, in_specs=in_specs, out_specs=out_specs, check_vma=False
    )
```

profile of v0, /device:TPU:0, one launch (start us, length us, event | category | flops | bytes accessed | tf_op | source)
XLA Modules:
  0.0 795.2 jit_solution(8337754750162333702)
XLA Ops:
  7.2 17.2 %convolution_bitcast_fusion.1 = f32[32,8,16,128]{3,2,1,0:T(8,128)S(1)} fusion(f32[1,32,8,128,128]{4,3,2,1,0:T(8,128)} %param.4), kind=kOutput, calls=%fused_computation.101 | convolution fusion | flops 805335040 | bytes 18874368 | tf_op jit(solution)/shard_map/cxyz,zk->cxky/dot_general | solution.py:34
  24.4 14.7 %negate_bitcast_fusion.1 = f32[32,8,16,128]{3,2,1,0:T(8,128)S(1)} fusion(f32[1,32,8,128,128]{4,3,2,1,0:T(8,128)S(1)} %copy-done.2), kind=kOutput, calls=%fused_computation.75 | convolution fusion | flops 805859328 | bytes 18874368 | tf_op jit(solution)/shard_map/cxyz,zk->cxky/dot_general | solution.py:35
  39.1 9.8 %fusion.57 = f32[32,32,8,16]{1,0,3,2:T(8,128)S(1)} fusion(f32[32,8,16,128]{3,2,1,0:T(8,128)S(1)} %negate_bitcast_fusion.1, s32[32]{0:T(128)S(1)} %compare_select_fusion), kind=kOutput, calls=%fused_computation.92 | convolution fusion | flops 201383936 | bytes 2621568 | tf_op jit(solution)/shard_map/cxky,yj->cxjk/dot_general | solution.py:39
  48.9 9.7 %fusion.59 = f32[32,32,8,16]{1,0,3,2:T(8,128)S(1)} fusion(f32[32,8,16,128]{3,2,1,0:T(8,128)S(1)} %negate_bitcast_fusion.1, s32[32]{0:T(128)S(1)} %compare_select_fusion), kind=kOutput, calls=%fused_computation.94 | convolution fusion | flops 201383936 | bytes 2621568 | tf_op jit(solution)/shard_map/cxky,yj->cxjk/dot_general | solution.py:36
  58.7 10.2 %add_bitcast_fusion.1 = f32[32,8,32,16]{0,2,3,1:T(8,128)S(1)} fusion(f32[32,32,8,16]{1,0,3,2:T(8,128)S(1)} %fusion.59, f32[32,8,16,128]{3,2,1,0:T(8,128)S(1)} %convolution_bitcast_fusion.1, s32[32]{0:T(128)S(1)} %compare_select_fusion), kind=kOutput, calls=%fused_computation.74 | convolution fusion | flops 201515008 | bytes 3145856 | tf_op jit(solution)/shard_map/cxky,yj->cxjk/dot_general | solution.py:36
  68.8 9.8 %subtract_bitcast_fusion.1 = f32[32,8,32,16]{0,2,3,1:T(8,128)S(1)} fusion(f32[32,32,8,16]{1,0,3,2:T(8,128)S(1)} %fusion.57, f32[32,8,16,128]{3,2,1,0:T(8,128)S(1)} %convolution_bitcast_fusion.1, s32[32]{0:T(128)S(1)} %compare_select_fusion), kind=kOutput, calls=%fused_computation.73 | convolution fusion | flops 201515008 | bytes 3145856 | tf_op jit(solution)/shard_map/cxky,yj->cxjk/dot_general | solution.py:39
  81.6 4.4 copy.335
  86.1 4.7 reshape.83
  90.8 7.4 all-to-all-start
  98.2 8.5 %fusion.393 = (f32[1,32,32,1024]{3,2,1,0:T(8,128)}, f32[1,32,32,1024]{3,2,1,0:T(8,128)}) fusion(f32[2,32,32,1024]{3,2,1,0:T(8,128)} %param.6), kind=kLoop, calls=%fused_computation.379 | loop fusion | bytes 16777216 | tf_op jit(solution)/shard_map/slice | solution.py:95
  106.7 11.6 %squeeze.39 = f32[32,32,32,32]{3,2,1,0:T(8,128)} reshape(f32[1,32,32,1024]{3,2,1,0:T(8,128)} %get-tuple-element.17) | data formatting | bytes 8388608 | tf_op jit(solution)/shard_map/squeeze | solution.py:95
  118.3 11.6 %squeeze.40 = f32[32,32,32,32]{3,2,1,0:T(8,128)} reshape(f32[1,32,32,1024]{3,2,1,0:T(8,128)} %get-tuple-element.18) | data formatting | bytes 8388608 | tf_op jit(solution)/shard_map/squeeze | solution.py:96
  136.5 6.6 copy.241
  152.8 3.6 fusion.76
  156.4 3.6 fusion.82
  160.0 12.7 %multiply_reduce_fusion.5 = (f32[32,32,32]{2,1,0:T(8,128)S(1)}, f32[32,32,32]{2,1,0:T(8,128)S(1)}, f32[32,32,32]{2,1,0:T(8,128)S(1)}, f32[32,32,32]{2,1,0:T(8,128)S(1)}) fusion(f32[32,32,32,32]{3,2,1,0:T(8,128)} %squeeze.40, f32[32,32,32]{1,0,2:T(8,128)S(1)} %fusion.76, f32[32,32,32]{1,0,2:T(8,128)S(1)} %fusion.82, f32[32,32,32,32]{3,2,1,0:T(8,128)} %squeeze.39), kind=kLoop, calls=%fused_computation.18 | loop fusion | flops 8257536 | bytes 9175040
  177.5 4.4 copy.130
  181.9 4.7 reshape.85
  186.7 6.0 all-to-all-start.1
  192.7 30.5 %fusion.10 = f32[32,8,128,128]{3,0,2,1:T(8,128)} fusion(f32[32,8,128,128]{3,2,1,0:T(8,128)} %bitcast.317, f32[32,32]{1,0:T(8,128)S(1)} %copy-done), kind=kOutput, calls=%fused_computation.24 | convolution fusion | flops 1610612736 | bytes 33558528 | tf_op jit(solution)/shard_map/co,cxyz->oxyz/dot_general | solution.py:110
  229.4 4.6 copy.333
  258.3 29.0 %fusion.38 = f32[32,8,128,128]{3,2,1,0:T(8,128)} fusion(f32[32,8,16,128]{3,2,1,0:T(8,128)S(1)} %fusion.156, f32[32,8,16,128]{3,2,1,0:T(8,128)S(1)} %copy-done.4, f32[16]{0:T(128)S(1)} %fusion.229), kind=kOutput, calls=%fused_computation.70 | convolution fusion | flops 806383616 | bytes 20971584 | tf_op jit(solution)/shard_map/cxky,zk->cxyz/dot_general | solution.py:79
  287.3 69.5 %fusion.6 = (f32[32,8,128,128]{3,2,1,0:T(8,128)S(1)}, f32[32,8,128,128]{3,2,1,0:T(8,128)}, f32[32,8,128,128]{3,2,1,0:T(8,128)}) fusion(f32[1,32,8,128,128]{4,3,2,1,0:T(8,128)} %param.5, f32[32,8,128,128]{3,0,2,1:T(8,128)} %fusion.10, f32[32,8,128,128]{3,2,1,0:T(8,128)} %fusion.38, f32[32,8,16,128]{3,2,1,0:T(8,128)S(1)} %fusion.142, ...), kind=kOutput, calls=%fused_computation.11 | convolution fusion | flops 1112567808 | bytes 104857664 | tf_op jit(solution)/shard_map/cxky,zk->cxyz/dot_general | solution.py:79
  356.9 14.6 %negate_bitcast_fusion = f32[32,8,16,128]{3,2,1,0:T(8,128)S(1)} fusion(f32[32,8,128,128]{3,2,1,0:T(8,128)S(1)} %get-tuple-element.15), kind=kOutput, calls=%fused_computation.67 | convolution fusion | flops 805859328 | bytes 18874368 | tf_op jit(solution)/shard_map/cxyz,zk->cxky/dot_general | solution.py:35
  371.4 14.8 %convolution_bitcast_fusion = f32[32,8,16,128]{3,2,1,0:T(8,128)S(1)} fusion(f32[32,8,128,128]{3,2,1,0:T(8,128)S(1)} %get-tuple-element.15), kind=kOutput, calls=%fused_computation.100 | convolution fusion | flops 805335040 | bytes 18874368 | tf_op jit(solution)/shard_map/cxyz,zk->cxky/dot_general | solution.py:34
  386.2 9.8 %fusion.45 = f32[32,32,8,16]{1,0,3,2:T(8,128)S(1)} fusion(f32[32,8,16,128]{3,2,1,0:T(8,128)S(1)} %negate_bitcast_fusion, s32[32]{0:T(128)S(1)} %copy-done.11), kind=kOutput, calls=%fused_computation.80 | convolution fusion | flops 201383936 | bytes 2621568 | tf_op jit(solution)/shard_map/cxky,yj->cxjk/dot_general | solution.py:39
  396.0 9.8 %fusion.47 = f32[32,32,8,16]{1,0,3,2:T(8,128)S(1)} fusion(f32[32,8,16,128]{3,2,1,0:T(8,128)S(1)} %negate_bitcast_fusion, s32[32]{0:T(128)S(1)} %copy-done.11), kind=kOutput, calls=%fused_computation.82 | convolution fusion | flops 201383936 | bytes 2621568 | tf_op jit(solution)/shard_map/cxky,yj->cxjk/dot_general | solution.py:36
  405.8 10.2 %multiply_bitcast_fusion.2 = f32[32,8,32,16]{0,2,3,1:T(8,128)S(1)} fusion(f32[32,32,8,16]{1,0,3,2:T(8,128)S(1)} %fusion.47, f32[32,8,16,128]{3,2,1,0:T(8,128)S(1)} %convolution_bitcast_fusion, f32[16]{0:T(128)S(1)} %fusion.229, s32[32]{0:T(128)S(1)} %copy-done.11), kind=kOutput, calls=%fused_computation.66 | convolution fusion | flops 201646080 | bytes 3145920 | tf_op jit(solution)/shard_map/cxky,yj->cxjk/dot_general | solution.py:36
  416.0 9.8 %multiply_bitcast_fusion.1 = f32[32,8,32,16]{0,2,3,1:T(8,128)S(1)} fusion(f32[32,32,8,16]{1,0,3,2:T(8,128)S(1)} %fusion.45, f32[32,8,16,128]{3,2,1,0:T(8,128)S(1)} %convolution_bitcast_fusion, f32[16]{0:T(128)S(1)} %fusion.229, s32[32]{0:T(128)S(1)} %copy-done.11), kind=kOutput, calls=%fused_computation.65 | convolution fusion | flops 201646080 | bytes 3145920 | tf_op jit(solution)/shard_map/cxky,yj->cxjk/dot_general | solution.py:39
  428.8 4.4 copy.334
  433.2 3.9 reshape.87
  437.1 30.6 %all_to_all.60 = f32[16,1,16384]{2,1,0:T(1,128)S(1)} all-to-all(f32[16,1,16384]{2,1,0:T(1,128)S(1)} %reshape.87), channel_id=1, replica_groups=mesh['dp'=2,'slab'=16] {'slab'}, dimensions={0} | all-to-all | bytes 2097152 | tf_op jit(solution)/shard_map/all_to_all | solution.py:115
  473.7 6.8 copy.243
  499.7 31.3 %add_bitcast_fusion = (f32[1,32,32,32,32]{4,3,2,1,0:T(8,128)}, f32[1,32,32,32,32]{4,3,2,1,0:T(8,128)}, f32[32,32,32]{1,0,2:T(8,128)S(1)}, f32[32,32,32]{1,0,2:T(...) fusion(f32[32,32,32]{2,1,0:T(8,128)} %copy.247, f32[32,32,32]{2,1,0:T(8,128)} %copy.246, ...), kind=kLoop, calls=%fused_computation.27 | loop fusion | flops 14548992 | bytes 17825792 | tf_op jit(solution)/shard_map/stack | solution.py:123
  531.0 24.1 %pad_maximum_fusion = f32[2,32,32,32,32]{4,3,2,1,0:T(8,128)} fusion(f32[1,32,32,32,32]{4,3,2,1,0:T(8,128)} %get-tuple-element.28, f32[1,32,32,32,32]{4,3,2,1,0:T(8,128)} %get-tuple-element.27), kind=kLoop, calls=%fused_computation | loop fusion | flops 2097152 | bytes 16777216 | tf_op jit(solution)/shard_map/stack | solution.py:123
  555.1 26.1 %reshape.58 = f32[2,32,32,1024]{3,2,1,0:T(8,128)} reshape(f32[2,32,32,32,32]{4,3,2,1,0:T(8,128)} %pad_maximum_fusion) | data formatting | bytes 16777216 | tf_op jit(solution)/shard_map/reshape | solution.py:124
  581.2 33.5 %fusion.8 = f32[8,128,128,32]{2,3,1,0:T(8,128)} fusion(f32[32,8,128,128]{3,2,1,0:T(8,128)} %copy-done.1, f32[32,32]{1,0:T(8,128)S(1)} %copy-done), kind=kOutput, calls=%fused_computation.21 | convolution fusion | flops 1610612736 | bytes 33558528 | tf_op jit(solution)/shard_map/co,oxyz->cxyz/dot_general | solution.py:134
  617.7 4.4 copy.155
  622.1 4.7 reshape.89
  626.8 5.0 all-to-all-start.3
  631.8 19.1 %multiply_bitcast_fusion = f32[1,32,8,128,128]{4,3,2,1,0:T(8,128)} fusion(f32[32,8,128,128]{3,2,1,0:T(8,128)} %get-tuple-element.16, f32[32,8,128,128]{3,2,1,0:T(8,128)} %get-tuple-element.33), kind=kLoop, calls=%fused_computation.28 | loop fusion | flops 8388608 | bytes 50331648 | tf_op jit(solution)/shard_map/broadcast_in_dim | solution.py:137
  650.9 3.8 all-to-all-done.3
  660.7 4.6 copy.332
  675.6 4.0 copy.158
  687.7 28.8 %fusion.34 = f32[32,8,128,128]{3,2,1,0:T(8,128)} fusion(f32[32,8,16,128]{3,2,1,0:T(8,128)S(1)} %fusion.150, f32[32,8,16,128]{3,2,1,0:T(8,128)S(1)} %fusion.138), kind=kOutput, calls=%fused_computation.63 | convolution fusion | flops 805859328 | bytes 20971520 | tf_op jit(solution)/shard_map/cxky,zk->cxyz/dot_general | solution.py:79
  716.6 45.4 %fusion.1 = f32[1,32,8,128,128]{4,3,2,1,0:T(8,128)} fusion(f32[8,128,128,32]{2,3,1,0:T(8,128)S(1)} %bitcast.319, f32[32,8,128,128]{3,2,1,0:T(8,128)} %fusion.34, f32[32,8,16,128]{3,2,1,0:T(8,128)S(1)} %fusion.136, f32[32,8,16,128]{3,2,1,0:T(8,128)S(1)} %fusion.148), kind=kOutput, calls=%fused_computation.4 | convolution fusion | flops 814247936 | bytes 54525952 | tf_op jit(solution)/shard_map/cxky,zk->cxyz/dot_general | solution.py:79
  762.0 17.6 %all-reduce.2.cloned.1.call-done = f32[2,32,32,1024]{3,2,1,0:T(8,128)} async-done(((f32[2,32,32,1024]{3,2,1,0:T(8,128)}), f32[2,32,32,1024]{3,2,1,0:T(8,128)}) %all-reduce.2.cloned.1.call-update) | async-done | bytes 8388624 | tf_op jit(solution)/shard_map/psum | solution.py:123
  779.6 8.4 %copy.337 = f32[2,32,32,1024]{3,2,1,0:T(8,128)} copy(f32[2,32,32,1024]{3,2,1,0:T(8,128)} %all-reduce.2.cloned.1.call-done) | data formatting | bytes 16777216
  (95 shorter events, 109.5 us)
Async XLA Ops:
  7.2 185.6 %copy-start = (f32[32,32]{1,0:T(8,128)S(1)}, f32[32,32]{1,0:T(8,128)}, u32[]{:S(2)}) copy-start(f32[32,32]{1,0:T(8,128)} %param.7) | copy-start | bytes 12292
  7.2 249.1 %copy-start.10 = (s32[32]{0:T(128)}, s32[32]{0:T(128)S(1)}, u32[]{:S(2)}) copy-start(s32[32]{0:T(128)S(1)} %compare_select_fusion) | copy-start | bytes 388
  7.2 17.2 %copy-start.2 = (f32[1,32,8,128,128]{4,3,2,1,0:T(8,128)S(1)}, f32[1,32,8,128,128]{4,3,2,1,0:T(8,128)}, u32[]{:S(2)}) copy-start(f32[1,32,8,128,128]{4,3,2,1,0:T(8,128)} %param.4) | copy-start | bytes 50331652
  90.8 39.2 %all-to-all-start = ((f32[16,1,16384]{2,1,0:T(1,128)}), f32[16,1,16384]{2,1,0:T(1,128)S(1)}, u32[]{:S(2)}, u32[]{:S(2)}) async-start(f32[16,1,16384]{2,1,0:T(1,128)} %reshape.83), calls=%async_computation | async-start | bytes 2097152 | tf_op jit(solution)/shard_map/all_to_all | solution.py:99
  156.4 16.3 %copy-start.5 = (f32[32,32,32]{1,0,2:T(8,128)}, f32[32,32,32]{1,0,2:T(8,128)S(1)}, u32[]{:S(2)}) copy-start(f32[32,32,32]{1,0,2:T(8,128)S(1)} %fusion.76) | copy-start | bytes 393220
  160.0 12.7 %copy-start.7 = (f32[32,32,32]{1,0,2:T(8,128)}, f32[32,32,32]{1,0,2:T(8,128)S(1)}, u32[]{:S(2)}) copy-start(f32[32,32,32]{1,0,2:T(8,128)S(1)} %fusion.82) | copy-start | bytes 393220
  186.7 36.6 %all-to-all-start.1 = ((f32[16,1,16384]{2,1,0:T(1,128)}), f32[16,1,16384]{2,1,0:T(1,128)S(1)}, u32[]{:S(2)}, u32[]{:S(2)}) async-start(f32[16,1,16384]{2,1,0:T(1,128)} %reshape.85), calls=%async_computation.1 | async-start | bytes 2097152 | tf_op jit(solution)/shard_map/all_to_all | solution.py:108
  192.7 587.0 %all-reduce.2.cloned.1.call-start = ((), (), s32[]{:S(2)}) async-start(), calls=%async_computation.4 | async-start | bytes 16777216 | tf_op jit(solution)/shard_map/psum | solution.py:123
  254.3 4.0 copy-start.4
  258.3 29.1 %copy-start.9 = (f32[32,8,16,128]{3,2,1,0:T(8,128)S(1)}, f32[32,8,16,128]{3,2,1,0:T(8,128)}, u32[]{:S(2)}) copy-start(f32[32,8,16,128]{3,2,1,0:T(8,128)} %fusion.154) | copy-start | bytes 6291460
  356.9 14.6 %copy-start.1 = (f32[32,8,128,128]{3,2,1,0:T(8,128)}, f32[32,8,128,128]{3,2,1,0:T(8,128)S(1)}, u32[]{:S(2)}) copy-start(f32[32,8,128,128]{3,2,1,0:T(8,128)S(1)} %get-tuple-element.15) | copy-start | bytes 50331652
  371.4 14.8 %copy-start.11 = (s32[32]{0:T(128)S(1)}, s32[32]{0:T(128)}, u32[]{:S(2)}) copy-start(s32[32]{0:T(128)} %copy-done.10) | copy-start | bytes 388
  490.3 9.5 %copy-start.6 = (f32[32,32,32]{1,0,2:T(8,128)S(1)}, f32[32,32,32]{1,0,2:T(8,128)}, u32[]{:S(2)}) copy-start(f32[32,32,32]{1,0,2:T(8,128)} %copy-done.5) | copy-start | bytes 393220
  490.3 9.4 %copy-start.8 = (f32[32,32,32]{1,0,2:T(8,128)S(1)}, f32[32,32,32]{1,0,2:T(8,128)}, u32[]{:S(2)}) copy-start(f32[32,32,32]{1,0,2:T(8,128)} %copy-done.7) | copy-start | bytes 393220
  626.8 28.0 %all-to-all-start.3 = ((f32[16,1,16384]{2,1,0:T(1,128)}), f32[16,1,16384]{2,1,0:T(1,128)S(1)}, u32[]{:S(2)}, u32[]{:S(2)}) async-start(f32[16,1,16384]{2,1,0:T(1,128)} %reshape.89), calls=%async_computation.3 | async-start | bytes 2097152 | tf_op jit(solution)/shard_map/all_to_all | solution.py:132
  679.7 4.0 copy-start.3
  685.7 30.9 %slice-start = ((s8[16777216]{0:T(1024)(128)(4,1)}), s8[4194304]{0:T(1024)(128)(4,1)S(1)}, s32[]{:S(2)}) async-start(s8[16777216]{0:T(1024)(128)(4,1)} %bitcast.318), calls=%async_computation.5 | async-start | bytes 8388608
  687.7 28.9 %slice-start.1 = ((s8[16777216]{0:T(1024)(128)(4,1)}), s8[4194304]{0:T(1024)(128)(4,1)S(1)}, s32[]{:S(2)}) async-start(s8[16777216]{0:T(1024)(128)(4,1)} %bitcast.318), calls=%async_computation.6 | async-start | bytes 8388608
  687.7 28.9 %slice-start.2 = ((s8[16777216]{0:T(1024)(128)(4,1)}), s8[4194304]{0:T(1024)(128)(4,1)S(1)}, s32[]{:S(2)}) async-start(s8[16777216]{0:T(1024)(128)(4,1)} %bitcast.318), calls=%async_computation.7 | async-start | bytes 8388608
  687.7 28.9 %slice-start.3 = ((s8[16777216]{0:T(1024)(128)(4,1)}), s8[4194304]{0:T(1024)(128)(4,1)S(1)}, s32[]{:S(2)}) async-start(s8[16777216]{0:T(1024)(128)(4,1)} %bitcast.318), calls=%async_computation.8 | async-start | bytes 8388608
Sparse Core Ops, SparseCore 0:
  581.3 198.3 all-reduce.1
where the time goes:
time: 802 us; the launch traced here: 795 us
  matrix products  430 us (54%)
  local copies, waits for them, and re-layouts  179 us (22%)
  other arithmetic  101 us (13%)
  blocking collectives  30.6 us (4%)
  waiting for transfers between devices  21.5 us (3%)
  starting transfers between devices  18.5 us (2%)
  between operations  15 us (2%)
    dot_general x2, matrix products, plane_inverse(): jnp.einsum('cxky,zk->cxyz', plane_im, z_sin, precision=precise)  115 us
    dot_general x2, matrix products, plane_inverse(): jnp.einsum('cxky,zk->cxyz', plane_re, z_cos, precision=precise)  57.9 us
    another operation x2, other arithmetic, on_device(): summed = lax.psum(jnp.stack([own_real, own_imag]), 'dp')  55.3 us
    unnamed x43, local copies, waits for them, and re-layouts  39.9 us
    dot_general x1, matrix products, on_device(): jnp.einsum('co,oxyz->cxyz', bypass_weight, grad_pre, precision=precise)  33.5 us
    dot_general x2, matrix products, plane_spectrum(): part_re = jnp.einsum('cxyz,zk->cxky', data, z_cos, precision=precise)  31.9 us
    all_to_all x1, blocking collectives, on_device(): lax.all_to_all(cot_spec, 'slab', split_axis=3, concat_axis=2, tiled=True)  30.6 us
    dot_general x1, matrix products, on_device(): jnp.einsum('co,cxyz->oxyz', bypass_weight, source, precision=precise)  30.5 us
  transfers between devices with their start and end apart: 4, of which 2 were waited for; matrix products, arithmetic and copies ran while one was open for 29% of the time, Pallas kernels for 0%

commit v1 on v0

--- a/solution.py
+++ b/solution.py
@@ -11,6 +11,18 @@
 KY = 32
 KZ = 16
 precise = lax.Precision.HIGHEST
+
+
+def exchange_directly(shard, axis, split, join):
+    ways, here = (lax.axis_size(axis), lax.axis_index(axis))
+    width = shard.shape[split] // ways
+    turned = jnp.roll(shard, -here * width, axis=split)
+    got = [lax.slice_in_dim(turned, 0, width, axis=split)]
+    for far in range(1, ways):
+        sent = lax.slice_in_dim(turned, far * width, (far + 1) * width, axis=split)
+        got.append(lax.ppermute(sent, axis, [(d, (d + far) % ways) for d in range(ways)]))
+    line = jnp.concatenate(got[::-1], axis=join)
+    return jnp.roll(line, (here + 1) * got[0].shape[join], axis=join)
 
 
 def wave_tables(length, count, signed):
@@ -112,7 +124,7 @@
     grad_pre = pullback(cotangent[0])[0]
     fold_grid = jnp.broadcast_to(fold, (KY, KZ))
     cot_spec = plane_spectrum(grad_pre, fold_grid, z_cos, z_sin, y_cos, y_sin)
-    cot_moved = lax.all_to_all(cot_spec, "slab", split_axis=3, concat_axis=2, tiled=True)
+    cot_moved = exchange_directly(cot_spec, "slab", 3, 2)
     grad_re, grad_im = along_first(cot_moved, x_cos, x_sin)
     own_real = jnp.einsum("cpi,opi->cpio", hat_re, grad_re, precision=precise) + jnp.einsum(
         "cpi,opi->cpio", hat_im, grad_im, precision=precise

time: 802 us -> 901 us (1.12)
  waiting for transfers between devices: 21.5 us -> 78.7 us
  local copies, waits for them, and re-layouts: 179 us -> 219 us
  starting transfers between devices: 18.5 us -> 54.4 us
  blocking collectives: 30.6 us -> 0 us
    ppermute x0 -> x15, waiting for transfers between devices: none -> 57.3 us  [exchange_directly(): lax.ppermute(sent, axis, [(d, (d + far) % ways) for d in range(ways)])]
    ppermute x0 -> x15, starting transfers between devices: none -> 35.1 us  [exchange_directly(): lax.ppermute(sent, axis, [(d, (d + far) % ways) for d in range(ways)])]
    ppermute x0 -> x15, local copies, waits for them, and re-layouts: none -> 31.8 us  [exchange_directly(): lax.ppermute(sent, axis, [(d, (d + far) % ways) for d in range(ways)])]
    all_to_all x1 -> x0, blocking collectives: 30.6 us -> none  [on_device(): lax.all_to_all(cot_spec, 'slab', split_axis=3, concat_axis=2, tiled=True)]
    concatenate x0 -> x1, local copies, waits for them, and re-layouts: none -> 21.8 us  [exchange_directly(): return jnp.roll(line, (here + 1) * got[0].shape[join], axis=join)]
    unnamed x43 -> x60, local copies, waits for them, and re-layouts: 39.9 us -> 35 us
  transfers between devices with their start and end apart: 4 -> 19, of which waited for: 2 -> 9; matrix products, arithmetic and copies ran while one was open for 29% -> 30% of each run, Pallas kernels for 0% -> 0%
where the time goes in v1:
time: 901 us; the launch traced here: 892 us
  matrix products  427 us (47%)
  local copies, waits for them, and re-layouts  219 us (24%)
  other arithmetic  97.6 us (11%)
  waiting for transfers between devices  78.7 us (9%)
  starting transfers between devices  54.4 us (6%)
  between operations  15.1 us (2%)
    dot_general x2, matrix products, plane_inverse(): jnp.einsum('cxky,zk->cxyz', plane_im, z_sin, precision=precise)  115 us
    dot_general x2, matrix products, plane_inverse(): jnp.einsum('cxky,zk->cxyz', plane_re, z_cos, precision=precise)  57.8 us
    ppermute x15, waiting for transfers between devices, exchange_directly(): lax.ppermute(sent, axis, [(d, (d + far) % ways) for d in range(ways)])  57.3 us
    another operation x2, other arithmetic, on_device(): summed = lax.psum(jnp.stack([own_real, own_imag]), 'dp')  55.3 us
    ppermute x15, starting transfers between devices, exchange_directly(): lax.ppermute(sent, axis, [(d, (d + far) % ways) for d in range(ways)])  35.1 us
    unnamed x60, local copies, waits for them, and re-layouts  35 us
    dot_general x1, matrix products, on_device(): jnp.einsum('co,oxyz->cxyz', bypass_weight, grad_pre, precision=precise)  33.5 us
    ppermute x15, local copies, waits for them, and re-layouts, exchange_directly(): lax.ppermute(sent, axis, [(d, (d + far) % ways) for d in range(ways)])  31.8 us
  transfers between devices with their start and end apart: 19, of which 9 were waited for; matrix products, arithmetic and copies ran while one was open for 30% of the time, Pallas kernels for 0%

profile of v1, /device:TPU:0, one launch (start us, length us, event | category | flops | bytes accessed | tf_op | source)
XLA Modules:
  0.0 892.4 jit_solution(18030049394877880007)
XLA Ops:
  7.2 17.2 %negate_bitcast_fusion.1 = f32[32,8,16,128]{3,2,1,0:T(8,128)S(1)} fusion(f32[1,32,8,128,128]{4,3,2,1,0:T(8,128)} %param.4), kind=kOutput, calls=%fused_computation.70 | convolution fusion | flops 805859328 | bytes 18874368 | tf_op jit(solution)/shard_map/cxyz,zk->cxky/dot_general | solution.py:47
  24.4 15.0 %convolution_bitcast_fusion.1 = f32[32,8,16,128]{3,2,1,0:T(8,128)S(1)} fusion(f32[1,32,8,128,128]{4,3,2,1,0:T(8,128)S(1)} %copy-done.2), kind=kOutput, calls=%fused_computation.92 | convolution fusion | flops 805335040 | bytes 18874368 | tf_op jit(solution)/shard_map/cxyz,zk->cxky/dot_general | solution.py:46
  39.5 9.8 %fusion.45 = f32[32,32,8,16]{1,0,3,2:T(8,128)S(1)} fusion(f32[32,8,16,128]{3,2,1,0:T(8,128)S(1)} %negate_bitcast_fusion.1, s32[32]{0:T(128)S(1)} %compare_select_fusion), kind=kOutput, calls=%fused_computation.83 | convolution fusion | flops 201383936 | bytes 2621568 | tf_op jit(solution)/shard_map/cxky,yj->cxjk/dot_general | solution.py:51
  49.2 9.7 %fusion.47 = f32[32,32,8,16]{1,0,3,2:T(8,128)S(1)} fusion(f32[32,8,16,128]{3,2,1,0:T(8,128)S(1)} %negate_bitcast_fusion.1, s32[32]{0:T(128)S(1)} %compare_select_fusion), kind=kOutput, calls=%fused_computation.85 | convolution fusion | flops 201383936 | bytes 2621568 | tf_op jit(solution)/shard_map/cxky,yj->cxjk/dot_general | solution.py:48
  59.0 10.0 %subtract_bitcast_fusion.1 = f32[32,8,32,16]{0,2,3,1:T(8,128)S(1)} fusion(f32[32,32,8,16]{1,0,3,2:T(8,128)S(1)} %fusion.45, f32[32,8,16,128]{3,2,1,0:T(8,128)S(1)} %convolution_bitcast_fusion.1, s32[32]{0:T(128)S(1)} %compare_select_fusion), kind=kOutput, calls=%fused_computation.68 | convolution fusion | flops 201515008 | bytes 3145856 | tf_op jit(solution)/shard_map/cxky,yj->cxjk/dot_general | solution.py:51
  70.2 10.2 %add_bitcast_fusion.1 = f32[32,8,32,16]{0,2,3,1:T(8,128)S(1)} fusion(f32[32,32,8,16]{1,0,3,2:T(8,128)S(1)} %fusion.47, f32[32,8,16,128]{3,2,1,0:T(8,128)S(1)} %convolution_bitcast_fusion.1, s32[32]{0:T(128)S(1)} %compare_select_fusion), kind=kOutput, calls=%fused_computation.69 | convolution fusion | flops 201515008 | bytes 3145856 | tf_op jit(solution)/shard_map/cxky,yj->cxjk/dot_general | solution.py:48
  81.9 4.4 copy.394
  86.4 4.7 reshape.79
  91.1 7.4 all-to-all-start
  98.5 8.5 fusion.376
  107.0 11.6 %squeeze.40 = f32[32,32,32,32]{3,2,1,0:T(8,128)} reshape(f32[1,32,32,1024]{3,2,1,0:T(8,128)} %get-tuple-element.18) | data formatting | bytes 8388608 | tf_op jit(solution)/shard_map/squeeze | solution.py:108
  118.7 11.7 %squeeze.39 = f32[32,32,32,32]{3,2,1,0:T(8,128)} reshape(f32[1,32,32,1024]{3,2,1,0:T(8,128)} %get-tuple-element.17) | data formatting | bytes 8388608 | tf_op jit(solution)/shard_map/squeeze | solution.py:107
  136.8 6.6 copy.310
  160.3 12.5 %multiply_reduce_fusion.5 = (f32[32,32,32]{2,1,0:T(8,128)S(1)}, f32[32,32,32]{2,1,0:T(8,128)S(1)}, f32[32,32,32]{2,1,0:T(8,128)S(1)}, f32[32,32,32]{2,1,0:T(8,128)S(1)}) fusion(f32[32,32,32,32]{3,2,1,0:T(8,128)} %squeeze.40, f32[32,32,32]{1,0,2:T(8,128)S(1)} %fusion.64, f32[32,32,32]{1,0,2:T(8,128)S(1)} %fusion.70, f32[32,32,32,32]{3,2,1,0:T(8,128)} %squeeze.39), kind=kLoop, calls=%fused_computation.18 | loop fusion | flops 8257536 | bytes 9175040
  182.0 4.7 reshape.81
  186.8 6.0 all-to-all-start.1
  192.9 30.7 %fusion.10 = f32[32,8,128,128]{3,0,2,1:T(8,128)} fusion(f32[32,8,128,128]{3,2,1,0:T(8,128)} %bitcast.301, f32[32,32]{1,0:T(8,128)S(1)} %copy-done), kind=kOutput, calls=%fused_computation.24 | convolution fusion | flops 1610612736 | bytes 33558528 | tf_op jit(solution)/shard_map/co,cxyz->oxyz/dot_general | solution.py:122
  229.7 4.6 copy.393
  258.4 29.0 %fusion.30 = f32[32,8,128,128]{3,2,1,0:T(8,128)} fusion(f32[32,8,16,128]{3,2,1,0:T(8,128)S(1)} %copy-done.4, f32[32,8,16,128]{3,2,1,0:T(8,128)S(1)} %fusion.127, f32[16]{0:T(128)S(1)} %fusion.252), kind=kOutput, calls=%fused_computation.65 | convolution fusion | flops 806383616 | bytes 20971584 | tf_op jit(solution)/shard_map/cxky,zk->cxyz/dot_general | solution.py:91
  287.4 69.7 %fusion.6 = (f32[32,8,128,128]{3,2,1,0:T(8,128)S(1)}, f32[32,8,128,128]{3,2,1,0:T(8,128)}, f32[32,8,128,128]{3,2,1,0:T(8,128)}) fusion(f32[1,32,8,128,128]{4,3,2,1,0:T(8,128)} %param.5, f32[32,8,128,128]{3,0,2,1:T(8,128)} %fusion.10, f32[32,8,128,128]{3,2,1,0:T(8,128)} %fusion.30, f32[32,8,16,128]{3,2,1,0:T(8,128)S(1)} %copy-done.9, ...), kind=kOutput, calls=%fused_computation.11 | convolution fusion | flops 1112567808 | bytes 104857664 | tf_op jit(solution)/shard_map/cxky,zk->cxyz/dot_general | solution.py:91
  357.1 14.6 %negate_bitcast_fusion = f32[32,8,16,128]{3,2,1,0:T(8,128)S(1)} fusion(f32[32,8,128,128]{3,2,1,0:T(8,128)S(1)} %get-tuple-element.15), kind=kOutput, calls=%fused_computation.62 | convolution fusion | flops 805859328 | bytes 18874368 | tf_op jit(solution)/shard_map/cxyz,zk->cxky/dot_general | solution.py:47
  371.7 14.7 %convolution_bitcast_fusion = f32[32,8,16,128]{3,2,1,0:T(8,128)S(1)} fusion(f32[32,8,128,128]{3,2,1,0:T(8,128)S(1)} %get-tuple-element.15), kind=kOutput, calls=%fused_computation.91 | convolution fusion | flops 805335040 | bytes 18874368 | tf_op jit(solution)/shard_map/cxyz,zk->cxky/dot_general | solution.py:46
  386.4 9.8 %fusion.35 = f32[32,32,8,16]{1,0,3,2:T(8,128)S(1)} fusion(f32[32,8,16,128]{3,2,1,0:T(8,128)S(1)} %negate_bitcast_fusion, s32[32]{0:T(128)S(1)} %copy-done.11), kind=kOutput, calls=%fused_computation.73 | convolution fusion | flops 201383936 | bytes 2621568 | tf_op jit(solution)/shard_map/cxky,yj->cxjk/dot_general | solution.py:48
  396.2 11.1 %fusion.33 = f32[32,32,8,16]{1,0,3,2:T(8,128)} fusion(f32[32,8,16,128]{3,2,1,0:T(8,128)S(1)} %negate_bitcast_fusion, s32[32]{0:T(128)S(1)} %copy-done.11), kind=kOutput, calls=%fused_computation.71 | convolution fusion | flops 201383936 | bytes 2621568 | tf_op jit(solution)/shard_map/cxky,yj->cxjk/dot_general | solution.py:51
  407.3 10.2 %multiply_bitcast_fusion.2 = f32[32,8,32,16]{0,2,3,1:T(8,128)S(1)} fusion(f32[32,32,8,16]{1,0,3,2:T(8,128)S(1)} %fusion.35, f32[32,8,16,128]{3,2,1,0:T(8,128)S(1)} %convolution_bitcast_fusion, f32[16]{0:T(128)S(1)} %fusion.252, s32[32]{0:T(128)S(1)} %copy-done.11), kind=kOutput, calls=%fused_computation.61 | convolution fusion | flops 201646080 | bytes 3145920 | tf_op jit(solution)/shard_map/cxky,yj->cxjk/dot_general | solution.py:48
  422.3 11.5 %multiply_bitcast_fusion.1 = f32[32,8,32,16]{0,2,3,1:T(8,128)S(1)} fusion(f32[32,32,8,16]{1,0,3,2:T(8,128)} %fusion.33, f32[32,8,16,128]{3,2,1,0:T(8,128)S(1)} %convolution_bitcast_fusion, f32[16]{0:T(128)S(1)} %fusion.252, s32[32]{0:T(128)S(1)} %copy-done.11), kind=kOutput, calls=%fused_computation.60 | convolution fusion | flops 201646080 | bytes 3145920 | tf_op jit(solution)/shard_map/cxky,yj->cxjk/dot_general | solution.py:51
  444.0 5.3 collective-permute-done
  449.3 5.6 collective-permute-done.1
  454.9 5.6 collective-permute-done.2
  460.6 5.6 collective-permute-done.3
  466.2 5.6 collective-permute-done.4
  471.8 5.6 collective-permute-done.5
  477.4 17.9 %collective-permute-start.10 = (f32[2,32,8,32]{3,2,1,0:T(8,128)}, f32[2,32,8,32]{3,2,1,0:T(8,128)}, u32[]{:S(2)}, u32[]{:S(2)}) collective-permute-start(f32[2,32,8,32]{3,2,1,0:T(8,128)} %get-tuple-element.35), channel_id=1, source_target_pairs={{0,5},{1,6},{2,7},{3,8},{4,9},{5,10},{6,11},{7,12},{8,13},{9,14},{... | collective-permute-start | bytes 196616 | tf_op jit(solution)/shard_map/ppermute | solution.py:23
  495.3 11.4 %collective-permute-start.11 = (f32[2,32,8,32]{3,2,1,0:T(8,128)}, f32[2,32,8,32]{3,2,1,0:T(8,128)}, u32[]{:S(2)}, u32[]{:S(2)}) collective-permute-start(f32[2,32,8,32]{3,2,1,0:T(8,128)} %get-tuple-element.34), channel_id=1, source_target_pairs={{0,4},{1,5},{2,6},{3,7},{4,8},{5,9},{6,10},{7,11},{8,12},{9,13},{1... | collective-permute-start | bytes 196616 | tf_op jit(solution)/shard_map/ppermute | solution.py:23
  506.6 24.0 %collective-permute-done.7 = f32[2,32,8,32]{3,2,1,0:T(8,128)S(1)} collective-permute-done((f32[2,32,8,32]{3,2,1,0:T(8,128)S(1)}, f32[2,32,8,32]{3,2,1,0:T(8,128)S(1)}, u32[]{:S(2)}, u32[]{:S(2)}) %collective-permute-start.7) | collective-permute-done | bytes 65568 | tf_op jit(solution)/shard_map/ppermute | solution.py:23
  564.3 21.8 %concatenate.13 = f32[2,32,256,32]{2,3,1,0:T(8,128)} concatenate(f32[2,32,8,32]{2,3,1,0:T(8,128)S(1)} %copy.198, f32[2,32,8,32]{2,3,1,0:T(8,128)S(1)} %copy.199, f32[2,32,8,32]{2,3,1,0:T(8,128)} %copy.200, f32[2,32,8,32]{2,3,1,0:T(8,128)} %copy.201, f32[2,32,8,32]{2,3,1,0:T(8,128)} %copy.202, f32[2,32,8,32]{2,3,1,0:T(8,128)} %copy.203, f32[2,32,8,32]{2,3,1,0:T(8,128)} %copy.204, ...), dimensions={2} | concatenate | bytes 4194304 | tf_op jit(solution)/shard_map/jit(_roll_dynamic)/concatenate | solution.py:25
  596.2 31.3 %add_bitcast_fusion = (f32[1,32,32,32,32]{4,3,2,1,0:T(8,128)}, f32[1,32,32,32,32]{4,3,2,1,0:T(8,128)}, f32[32,32,32]{1,0,2:T(8,128)S(1)}, f32[32,32,32]{1,0,2:T(...) fusion(f32[32,32,32]{2,1,0:T(8,128)} %copy.332, f32[32,32,32]{2,1,0:T(8,128)} %copy.331, ...), kind=kLoop, calls=%fused_computation.27 | loop fusion | flops 14548992 | bytes 17825792 | tf_op jit(solution)/shard_map/stack | solution.py:135
  627.5 24.1 %pad_maximum_fusion = f32[2,32,32,32,32]{4,3,2,1,0:T(8,128)} fusion(f32[1,32,32,32,32]{4,3,2,1,0:T(8,128)} %get-tuple-element.26, f32[1,32,32,32,32]{4,3,2,1,0:T(8,128)} %get-tuple-element.25), kind=kLoop, calls=%fused_computation | loop fusion | flops 2097152 | bytes 16777216 | tf_op jit(solution)/shard_map/stack | solution.py:135
  651.5 26.1 %reshape.54 = f32[2,32,32,1024]{3,2,1,0:T(8,128)} reshape(f32[2,32,32,32,32]{4,3,2,1,0:T(8,128)} %pad_maximum_fusion) | data formatting | bytes 16777216 | tf_op jit(solution)/shard_map/reshape | solution.py:136
  677.6 33.5 %fusion.8 = f32[8,128,128,32]{2,3,1,0:T(8,128)} fusion(f32[32,8,128,128]{3,2,1,0:T(8,128)} %copy-done.1, f32[32,32]{1,0:T(8,128)S(1)} %copy-done), kind=kOutput, calls=%fused_computation.21 | convolution fusion | flops 1610612736 | bytes 33558528 | tf_op jit(solution)/shard_map/co,oxyz->cxyz/dot_general | solution.py:146
  718.5 4.7 reshape.83
  723.3 5.8 all-to-all-start.2
  729.1 19.1 %multiply_bitcast_fusion = f32[1,32,8,128,128]{4,3,2,1,0:T(8,128)} fusion(f32[32,8,128,128]{3,2,1,0:T(8,128)} %get-tuple-element.16, f32[32,8,128,128]{3,2,1,0:T(8,128)} %get-tuple-element.47), kind=kLoop, calls=%fused_computation.28 | loop fusion | flops 8388608 | bytes 50331648 | tf_op jit(solution)/shard_map/broadcast_in_dim | solution.py:149
  757.9 4.6 copy.392
  785.2 28.8 %fusion.26 = f32[32,8,128,128]{3,2,1,0:T(8,128)} fusion(f32[32,8,16,128]{3,2,1,0:T(8,128)S(1)} %fusion.133, f32[32,8,16,128]{3,2,1,0:T(8,128)S(1)} %fusion.121), kind=kOutput, calls=%fused_computation.58 | convolution fusion | flops 805859328 | bytes 20971520 | tf_op jit(solution)/shard_map/cxky,zk->cxyz/dot_general | solution.py:91
  814.0 45.4 %fusion.1 = f32[1,32,8,128,128]{4,3,2,1,0:T(8,128)} fusion(f32[8,128,128,32]{2,3,1,0:T(8,128)S(1)} %bitcast.303, f32[32,8,128,128]{3,2,1,0:T(8,128)} %fusion.26, f32[32,8,16,128]{3,2,1,0:T(8,128)S(1)} %fusion.119, f32[32,8,16,128]{3,2,1,0:T(8,128)S(1)} %fusion.131), kind=kOutput, calls=%fused_computation.4 | convolution fusion | flops 814247936 | bytes 54525952 | tf_op jit(solution)/shard_map/cxky,zk->cxyz/dot_general | solution.py:91
  859.4 17.5 %all-reduce.2.cloned.1.call-done = f32[2,32,32,1024]{3,2,1,0:T(8,128)} async-done(((f32[2,32,32,1024]{3,2,1,0:T(8,128)}), f32[2,32,32,1024]{3,2,1,0:T(8,128)}) %all-reduce.2.cloned.1.call-update) | async-done | bytes 8388624 | tf_op jit(solution)/shard_map/psum | solution.py:135
  876.9 8.4 copy.396
  (156 shorter events, 163.7 us)
Async XLA Ops:
  7.2 185.7 %copy-start = (f32[32,32]{1,0:T(8,128)S(1)}, f32[32,32]{1,0:T(8,128)}, u32[]{:S(2)}) copy-start(f32[32,32]{1,0:T(8,128)} %param.7) | copy-start | bytes 12292
  7.2 249.2 %copy-start.10 = (s32[32]{0:T(128)}, s32[32]{0:T(128)S(1)}, u32[]{:S(2)}) copy-start(s32[32]{0:T(128)S(1)} %compare_select_fusion) | copy-start | bytes 388
  7.2 17.2 %copy-start.2 = (f32[1,32,8,128,128]{4,3,2,1,0:T(8,128)S(1)}, f32[1,32,8,128,128]{4,3,2,1,0:T(8,128)}, u32[]{:S(2)}) copy-start(f32[1,32,8,128,128]{4,3,2,1,0:T(8,128)} %param.4) | copy-start | bytes 50331652
  91.1 39.2 %all-to-all-start = ((f32[16,1,16384]{2,1,0:T(1,128)}), f32[16,1,16384]{2,1,0:T(1,128)S(1)}, u32[]{:S(2)}, u32[]{:S(2)}) async-start(f32[16,1,16384]{2,1,0:T(1,128)} %reshape.79), calls=%async_computation | async-start | bytes 2097152 | tf_op jit(solution)/shard_map/all_to_all | solution.py:111
  156.7 16.1 %copy-start.5 = (f32[32,32,32]{1,0,2:T(8,128)}, f32[32,32,32]{1,0,2:T(8,128)S(1)}, u32[]{:S(2)}) copy-start(f32[32,32,32]{1,0,2:T(8,128)S(1)} %fusion.64) | copy-start | bytes 393220
  160.3 12.5 %copy-start.7 = (f32[32,32,32]{1,0,2:T(8,128)}, f32[32,32,32]{1,0,2:T(8,128)S(1)}, u32[]{:S(2)}) copy-start(f32[32,32,32]{1,0,2:T(8,128)S(1)} %fusion.70) | copy-start | bytes 393220
  186.8 36.9 %all-to-all-start.1 = ((f32[16,1,16384]{2,1,0:T(1,128)}), f32[16,1,16384]{2,1,0:T(1,128)S(1)}, u32[]{:S(2)}, u32[]{:S(2)}) async-start(f32[16,1,16384]{2,1,0:T(1,128)} %reshape.81), calls=%async_computation.1 | async-start | bytes 2097152 | tf_op jit(solution)/shard_map/all_to_all | solution.py:120
  192.8 684.1 %all-reduce.2.cloned.1.call-start = ((), (), s32[]{:S(2)}) async-start(), calls=%async_computation.3 | async-start | bytes 16777216 | tf_op jit(solution)/shard_map/psum | solution.py:135
  254.3 4.0 copy-start.4
  258.4 29.0 %copy-start.9 = (f32[32,8,16,128]{3,2,1,0:T(8,128)S(1)}, f32[32,8,16,128]{3,2,1,0:T(8,128)}, u32[]{:S(2)}) copy-start(f32[32,8,16,128]{3,2,1,0:T(8,128)} %fusion.125) | copy-start | bytes 6291460
  357.1 14.6 %copy-start.1 = (f32[32,8,128,128]{3,2,1,0:T(8,128)}, f32[32,8,128,128]{3,2,1,0:T(8,128)S(1)}, u32[]{:S(2)}) copy-start(f32[32,8,128,128]{3,2,1,0:T(8,128)S(1)} %get-tuple-element.15) | copy-start | bytes 50331652
  371.7 14.7 %copy-start.11 = (s32[32]{0:T(128)S(1)}, s32[32]{0:T(128)}, u32[]{:S(2)}) copy-start(s32[32]{0:T(128)} %copy-done.10) | copy-start | bytes 388
  438.2 11.1 %collective-permute-start = (f32[2,32,8,32]{3,2,1,0:T(8,128)S(1)}, f32[2,32,8,32]{3,2,1,0:T(8,128)S(1)}, u32[]{:S(2)}, u32[]{:S(2)}) collective-permute-start(f32[2,32,8,32]{3,2,1,0:T(8,128)S(1)} %get-tuple-element.45), channel_id=1, source_target_pairs={{0,15},{1,0},{2,1},{3,2},{4,3},{5,4},{6,5},{7,6},{8,7},{9,8},{10,9... | collective-permute-start | bytes 196616 | tf_op jit(solution)/shard_map/ppermute | solution.py:23
  442.6 12.4 %collective-permute-start.1 = (f32[2,32,8,32]{3,2,1,0:T(8,128)S(1)}, f32[2,32,8,32]{3,2,1,0:T(8,128)S(1)}, u32[]{:S(2)}, u32[]{:S(2)}) collective-permute-start(f32[2,32,8,32]{3,2,1,0:T(8,128)S(1)} %get-tuple-element.44), channel_id=1, source_target_pairs={{0,14},{1,15},{2,0},{3,1},{4,2},{5,3},{6,4},{7,5},{8,6},{9,7},{10,... | collective-permute-start | bytes 196616 | tf_op jit(solution)/shard_map/ppermute | solution.py:23
  443.1 17.4 %collective-permute-start.2 = (f32[2,32,8,32]{3,2,1,0:T(8,128)S(1)}, f32[2,32,8,32]{3,2,1,0:T(8,128)S(1)}, u32[]{:S(2)}, u32[]{:S(2)}) collective-permute-start(f32[2,32,8,32]{3,2,1,0:T(8,128)S(1)} %get-tuple-element.43), channel_id=1, source_target_pairs={{0,13},{1,14},{2,15},{3,0},{4,1},{5,2},{6,3},{7,4},{8,5},{9,6},{10... | collective-permute-start | bytes 196616 | tf_op jit(solution)/shard_map/ppermute | solution.py:23
  443.2 23.0 %collective-permute-start.3 = (f32[2,32,8,32]{3,2,1,0:T(8,128)S(1)}, f32[2,32,8,32]{3,2,1,0:T(8,128)S(1)}, u32[]{:S(2)}, u32[]{:S(2)}) collective-permute-start(f32[2,32,8,32]{3,2,1,0:T(8,128)S(1)} %get-tuple-element.42), channel_id=1, source_target_pairs={{0,12},{1,13},{2,14},{3,15},{4,0},{5,1},{6,2},{7,3},{8,4},{9,5},{1... | collective-permute-start | bytes 196616 | tf_op jit(solution)/shard_map/ppermute | solution.py:23
  443.8 28.0 %collective-permute-start.4 = (f32[2,32,8,32]{3,2,1,0:T(8,128)S(1)}, f32[2,32,8,32]{3,2,1,0:T(8,128)S(1)}, u32[]{:S(2)}, u32[]{:S(2)}) collective-permute-start(f32[2,32,8,32]{3,2,1,0:T(8,128)S(1)} %get-tuple-element.41), channel_id=1, source_target_pairs={{0,11},{1,12},{2,13},{3,14},{4,15},{5,0},{6,1},{7,2},{8,3},{9,4},{... | collective-permute-start | bytes 196616 | tf_op jit(solution)/shard_map/ppermute | solution.py:23
  449.3 28.1 %collective-permute-start.5 = (f32[2,32,8,32]{3,2,1,0:T(8,128)S(1)}, f32[2,32,8,32]{3,2,1,0:T(8,128)S(1)}, u32[]{:S(2)}, u32[]{:S(2)}) collective-permute-start(f32[2,32,8,32]{3,2,1,0:T(8,128)S(1)} %get-tuple-element.40), channel_id=1, source_target_pairs={{0,10},{1,11},{2,12},{3,13},{4,14},{5,15},{6,0},{7,1},{8,2},{9,3},... | collective-permute-start | bytes 196616 | tf_op jit(solution)/shard_map/ppermute | solution.py:23
  454.9 77.1 %copy-start.12 = (f32[2,32,8,32]{3,2,1,0:T(8,128)}, f32[2,32,8,32]{3,2,1,0:T(8,128)S(1)}, u32[]{:S(2)}) copy-start(f32[2,32,8,32]{3,2,1,0:T(8,128)S(1)} %collective-permute-done.1) | copy-start | bytes 196612
  454.9 40.3 %collective-permute-start.6 = (f32[2,32,8,32]{3,2,1,0:T(8,128)S(1)}, f32[2,32,8,32]{3,2,1,0:T(8,128)S(1)}, u32[]{:S(2)}, u32[]{:S(2)}) collective-permute-start(f32[2,32,8,32]{3,2,1,0:T(8,128)S(1)} %get-tuple-element.39), channel_id=1, source_target_pairs={{0,9},{1,10},{2,11},{3,12},{4,13},{5,14},{6,15},{7,0},{8,1},{9,2},... | collective-permute-start | bytes 196616 | tf_op jit(solution)/shard_map/ppermute | solution.py:23
  460.5 71.5 %copy-start.13 = (f32[2,32,8,32]{3,2,1,0:T(8,128)}, f32[2,32,8,32]{3,2,1,0:T(8,128)S(1)}, u32[]{:S(2)}) copy-start(f32[2,32,8,32]{3,2,1,0:T(8,128)S(1)} %collective-permute-done.2) | copy-start | bytes 196612
  460.5 70.1 %collective-permute-start.7 = (f32[2,32,8,32]{3,2,1,0:T(8,128)S(1)}, f32[2,32,8,32]{3,2,1,0:T(8,128)S(1)}, u32[]{:S(2)}, u32[]{:S(2)}) collective-permute-start(f32[2,32,8,32]{3,2,1,0:T(8,128)S(1)} %get-tuple-element.38), channel_id=1, source_target_pairs={{0,8},{1,9},{2,10},{3,11},{4,12},{5,13},{6,14},{7,15},{8,0},{9,1},... | collective-permute-start | bytes 196616 | tf_op jit(solution)/shard_map/ppermute | solution.py:23
  466.2 65.9 %copy-start.14 = (f32[2,32,8,32]{3,2,1,0:T(8,128)}, f32[2,32,8,32]{3,2,1,0:T(8,128)S(1)}, u32[]{:S(2)}) copy-start(f32[2,32,8,32]{3,2,1,0:T(8,128)S(1)} %collective-permute-done.3) | copy-start | bytes 196612
  466.2 64.5 %collective-permute-start.8 = (f32[2,32,8,32]{3,2,1,0:T(8,128)S(1)}, f32[2,32,8,32]{3,2,1,0:T(8,128)S(1)}, u32[]{:S(2)}, u32[]{:S(2)}) collective-permute-start(f32[2,32,8,32]{3,2,1,0:T(8,128)S(1)} %get-tuple-element.37), channel_id=1, source_target_pairs={{0,7},{1,8},{2,9},{3,10},{4,11},{5,12},{6,13},{7,14},{8,15},{9,0},... | collective-permute-start | bytes 196616 | tf_op jit(solution)/shard_map/ppermute | solution.py:23
  471.8 60.6 %copy-start.15 = (f32[2,32,8,32]{3,2,1,0:T(8,128)}, f32[2,32,8,32]{3,2,1,0:T(8,128)S(1)}, u32[]{:S(2)}) copy-start(f32[2,32,8,32]{3,2,1,0:T(8,128)S(1)} %collective-permute-done.4) | copy-start | bytes 196612
  471.8 58.9 %collective-permute-start.9 = (f32[2,32,8,32]{3,2,1,0:T(8,128)S(1)}, f32[2,32,8,32]{3,2,1,0:T(8,128)S(1)}, u32[]{:S(2)}, u32[]{:S(2)}) collective-permute-start(f32[2,32,8,32]{3,2,1,0:T(8,128)S(1)} %get-tuple-element.36), channel_id=1, source_target_pairs={{0,6},{1,7},{2,8},{3,9},{4,10},{5,11},{6,12},{7,13},{8,14},{9,15},... | collective-permute-start | bytes 196616 | tf_op jit(solution)/shard_map/ppermute | solution.py:23
  477.4 55.0 %copy-start.16 = (f32[2,32,8,32]{3,2,1,0:T(8,128)}, f32[2,32,8,32]{3,2,1,0:T(8,128)S(1)}, u32[]{:S(2)}) copy-start(f32[2,32,8,32]{3,2,1,0:T(8,128)S(1)} %collective-permute-done.5) | copy-start | bytes 196612
  477.4 75.2 %collective-permute-start.10 = (f32[2,32,8,32]{3,2,1,0:T(8,128)}, f32[2,32,8,32]{3,2,1,0:T(8,128)}, u32[]{:S(2)}, u32[]{:S(2)}) collective-permute-start(f32[2,32,8,32]{3,2,1,0:T(8,128)} %get-tuple-element.35), channel_id=1, source_target_pairs={{0,5},{1,6},{2,7},{3,8},{4,9},{5,10},{6,11},{7,12},{8,13},{9,14},{... | collective-permute-start | bytes 196616 | tf_op jit(solution)/shard_map/ppermute | solution.py:23
  495.3 37.2 %copy-start.17 = (f32[2,32,8,32]{3,2,1,0:T(8,128)}, f32[2,32,8,32]{3,2,1,0:T(8,128)S(1)}, u32[]{:S(2)}) copy-start(f32[2,32,8,32]{3,2,1,0:T(8,128)S(1)} %collective-permute-done.6) | copy-start | bytes 196612
  495.3 59.7 %collective-permute-start.11 = (f32[2,32,8,32]{3,2,1,0:T(8,128)}, f32[2,32,8,32]{3,2,1,0:T(8,128)}, u32[]{:S(2)}, u32[]{:S(2)}) collective-permute-start(f32[2,32,8,32]{3,2,1,0:T(8,128)} %get-tuple-element.34), channel_id=1, source_target_pairs={{0,4},{1,5},{2,6},{3,7},{4,8},{5,9},{6,10},{7,11},{8,12},{9,13},{1... | collective-permute-start | bytes 196616 | tf_op jit(solution)/shard_map/ppermute | solution.py:23
  530.6 0.7 copy-start.18
  530.6 26.7 %collective-permute-start.12 = (f32[2,32,8,32]{3,2,1,0:T(8,128)}, f32[2,32,8,32]{3,2,1,0:T(8,128)}, u32[]{:S(2)}, u32[]{:S(2)}) collective-permute-start(f32[2,32,8,32]{3,2,1,0:T(8,128)} %get-tuple-element.33), channel_id=1, source_target_pairs={{0,3},{1,4},{2,5},{3,6},{4,7},{5,8},{6,9},{7,10},{8,11},{9,12},{10... | collective-permute-start | bytes 196616 | tf_op jit(solution)/shard_map/ppermute | solution.py:23
  530.6 0.8 copy-start.19
  530.6 29.0 %collective-permute-start.13 = (f32[2,32,8,32]{3,2,1,0:T(8,128)}, f32[2,32,8,32]{3,2,1,0:T(8,128)}, u32[]{:S(2)}, u32[]{:S(2)}) collective-permute-start(f32[2,32,8,32]{3,2,1,0:T(8,128)} %get-tuple-element.32), channel_id=1, source_target_pairs={{0,2},{1,3},{2,4},{3,5},{4,6},{5,7},{6,8},{7,9},{8,10},{9,11},{10,... | collective-permute-start | bytes 196616 | tf_op jit(solution)/shard_map/ppermute | solution.py:23
  531.3 0.7 copy-start.20
  532.0 29.9 %collective-permute-start.14 = (f32[2,32,8,32]{3,2,1,0:T(8,128)S(1)}, f32[2,32,8,32]{3,2,1,0:T(8,128)}, u32[]{:S(2)}, u32[]{:S(2)}) collective-permute-start(f32[2,32,8,32]{3,2,1,0:T(8,128)S(1)} %get-tuple-element.46), channel_id=1, source_target_pairs={{0,1},{1,2},{2,3},{3,4},{4,5},{5,6},{6,7},{7,8},{8,9},{9,10},{10,1... | collective-permute-start | bytes 196616 | tf_op jit(solution)/shard_map/ppermute | solution.py:23
  586.1 10.1 %copy-start.6 = (f32[32,32,32]{1,0,2:T(8,128)S(1)}, f32[32,32,32]{1,0,2:T(8,128)}, u32[]{:S(2)}) copy-start(f32[32,32,32]{1,0,2:T(8,128)} %copy-done.5) | copy-start | bytes 393220
  586.1 10.1 %copy-start.8 = (f32[32,32,32]{1,0,2:T(8,128)S(1)}, f32[32,32,32]{1,0,2:T(8,128)}, u32[]{:S(2)}) copy-start(f32[32,32,32]{1,0,2:T(8,128)} %copy-done.7) | copy-start | bytes 393220
  723.3 28.7 %all-to-all-start.2 = ((f32[16,1,16384]{2,1,0:T(1,128)}), f32[16,1,16384]{2,1,0:T(1,128)S(1)}, u32[]{:S(2)}, u32[]{:S(2)}) async-start(f32[16,1,16384]{2,1,0:T(1,128)} %reshape.83), calls=%async_computation.2 | async-start | bytes 2097152 | tf_op jit(solution)/shard_map/all_to_all | solution.py:144
  777.1 4.0 copy-start.3
  783.1 30.9 %slice-start = ((s8[16777216]{0:T(1024)(128)(4,1)}), s8[4194304]{0:T(1024)(128)(4,1)S(1)}, s32[]{:S(2)}) async-start(s8[16777216]{0:T(1024)(128)(4,1)} %bitcast.302), calls=%async_computation.4 | async-start | bytes 8388608
  785.1 28.9 %slice-start.1 = ((s8[16777216]{0:T(1024)(128)(4,1)}), s8[4194304]{0:T(1024)(128)(4,1)S(1)}, s32[]{:S(2)}) async-start(s8[16777216]{0:T(1024)(128)(4,1)} %bitcast.302), calls=%async_computation.5 | async-start | bytes 8388608
  785.2 28.8 %slice-start.2 = ((s8[16777216]{0:T(1024)(128)(4,1)}), s8[4194304]{0:T(1024)(128)(4,1)S(1)}, s32[]{:S(2)}) async-start(s8[16777216]{0:T(1024)(128)(4,1)} %bitcast.302), calls=%async_computation.6 | async-start | bytes 8388608
  785.2 28.8 %slice-start.3 = ((s8[16777216]{0:T(1024)(128)(4,1)}), s8[4194304]{0:T(1024)(128)(4,1)S(1)}, s32[]{:S(2)}) async-start(s8[16777216]{0:T(1024)(128)(4,1)} %bitcast.302), calls=%async_computation.7 | async-start | bytes 8388608
Sparse Core Ops, SparseCore 0:
  677.7 199.1 all-reduce.1
